TPU v7x, 32 devices: a whole 2x2x4 slice. The times are simulated.
32 devices in a mesh: chan: 4 (over y, core), tm: 8 (over z, x).
Axes of the slice: x: 2, y: 2, z: 4, core: 2. Of those that a mesh axis runs over, the one named last changes fastest.
Arguments:
- record: bfloat16 [2048, 16, 2560], P('chan', 'tm'), may hold values from -6 to 6
- partners: int32 [2048, 8], P('chan'), may hold values from 0 to 2047, as said below
- block_owner: int32 [4, 8], P('chan'), may hold values from 0 to 7, each once within a row
Outputs:
- stacks: float32 [16384, 257], P(('chan', 'tm'))
Inputs may be any that keep to these rules, and one draw needn't show every extreme that they name: `partners`: every partner is another channel at most 512 channels away; in every channel block one channel has a partner exactly 512 away. `block_owner`: each row names every index of tm once.
All inputs are finite; a program needn't handle non-finite values.
Results may differ from a plain program's by a relative error of at most 0.0028.
Values may be sent and summed in bfloat16 or wider, within the bound.
A program may use at most 128 MiB of HBM per device.

v0:
```python
import math

import jax
import jax.numpy as jnp
from jax import lax
from jax.sharding import PartitionSpec as P

NFB = 512
F0 = 64
K = 8
LAG = 128


def extended(array, sides, width):
    for axis, dim in sides:
        size, length = (lax.axis_size(axis), array.shape[dim])
        up = [(i, (i + 1) % size) for i in range(size - 1)]
        down = [(j, i) for i, j in up]
        last = lax.slice_in_dim(array, length - width, length, axis=dim)
        first = lax.slice_in_dim(array, 0, width, axis=dim)
        before = lax.ppermute(last, axis, up)
        after = lax.ppermute(first, axis, down)
        array = jnp.concatenate([before, array, after], axis=dim)
    return array


def fourier_table(samples):
    times = jnp.arange(samples, dtype=jnp.int32)[:, None]
    freqs = (F0 + jnp.arange(NFB, dtype=jnp.int32))[None, :]
    phase = (times * freqs % (2 * samples)).astype(jnp.float32) * (2.0 * math.pi / (2 * samples))
    return jnp.concatenate([jnp.cos(phase), -jnp.sin(phase)], axis=1).astype(jnp.bfloat16)


def lag_table(samples):
    freqs = (F0 + jnp.arange(NFB, dtype=jnp.int32))[:, None]
    shifts = (jnp.arange(2 * LAG + 1, dtype=jnp.int32) - LAG)[None, :]
    phase = (freqs * shifts % (2 * samples)).astype(jnp.float32) * (2.0 * math.pi / (2 * samples))
    return jnp.concatenate([jnp.cos(phase), -jnp.sin(phase)], axis=0)


def whiten(rows, fourier):
    samples = rows.shape[2]
    flat = rows.reshape(-1, samples)
    spectra = jnp.dot(flat, fourier, preferred_element_type=jnp.float32)
    real_part = spectra[:, :NFB]
    imag_part = spectra[:, NFB:]
    energy = real_part * real_part + imag_part * imag_part
    level = jnp.mean(energy, axis=1, keepdims=True)
    divisor = jnp.sqrt(energy + 0.1 * level + 1e-05)
    whitened = jnp.concatenate([real_part / divisor, imag_part / divisor], axis=1)
    return whitened.astype(jnp.bfloat16).reshape(rows.shape[0], rows.shape[1], 2 * NFB)


def shards(record, partners, block_owner):
    block_size, windows_dev, samples = record.shape
    fourier = fourier_table(samples)
    widened = extended(record, (("chan", 0),), block_size)
    whitened = whiten(widened, fourier)
    base_row = lax.axis_index("chan") * block_size - block_size
    local_rows = (partners - base_row).reshape(-1)
    partner_rows = jnp.take(whitened, local_rows, axis=0).reshape(
        block_size, K, windows_dev, 2 * NFB
    )
    own_rows = whitened[block_size : 2 * block_size]
    own_real = own_rows[:, None, :, :NFB].astype(jnp.float32)
    own_imag = own_rows[:, None, :, NFB:].astype(jnp.float32)
    far_real = partner_rows[:, :, :, :NFB].astype(jnp.float32)
    far_imag = partner_rows[:, :, :, NFB:].astype(jnp.float32)
    cross_real = jnp.sum(own_real * far_real + own_imag * far_imag, axis=2)
    cross_imag = jnp.sum(own_real * far_imag - own_imag * far_real, axis=2)
    cross = jnp.concatenate([cross_real, cross_imag], axis=2).reshape(block_size * K, 2 * NFB)
    tm_count = lax.axis_size("tm")
    block_rows = block_size * K // tm_count
    owner_row = block_owner[0]
    onehot = (owner_row[None, :] == jnp.arange(tm_count, dtype=jnp.int32)[:, None]).astype(
        jnp.int32
    )
    inverse = jnp.sum(onehot * jnp.arange(tm_count, dtype=jnp.int32)[None, :], axis=1)
    ordered = jnp.take(cross.reshape(tm_count, block_rows, 2 * NFB), inverse, axis=0).reshape(
        -1, 2 * NFB
    )
    lag_weights = lag_table(samples)
    scale = 1.0 / math.sqrt(windows_dev * tm_count * NFB)
    summed = lax.psum_scatter(
        ordered.astype(jnp.bfloat16), "tm", scatter_dimension=0, tiled=True
    ).astype(jnp.float32)
    stacked = jnp.dot(
        summed, lag_weights, precision=lax.Precision.HIGHEST, preferred_element_type=jnp.float32
    )
    return stacked * scale


def solution(mesh):
    placed = (P("chan", "tm", None), P("chan", None), P("chan", None))
    return jax.shard_map(
        shards, mesh=mesh, in_specs=placed, out_specs=P(("chan", "tm"), None), check_vma=False
    )
```

profile of v0, /device:TPU:11, one launch (start us, length us, event | category | flops | bytes accessed | tf_op | source)
XLA Modules:
  0.0 547.9 jit_solution(10894492011192457910)
XLA Ops:
  6.5 0.0 reduce-scatter.2.cloned.1.call-start
  6.5 2.6 collective-permute-start.1
  9.1 3.0 collective-permute-start
  12.2 0.7 compare_and_fusion
  12.9 0.1 copy.8
  13.0 0.2 reshape.91
  13.2 0.2 copy.7
  13.4 0.0 copy-start.4
  13.4 0.9 select_reduce_fusion
  14.3 0.1 broadcast_bitcast_fusion
  14.5 23.0 %cosine_convert_fusion = (bf16[2560,512]{1,0:T(8,128)(2,1)S(1)}, bf16[2560,512]{1,0:T(8,128)(2,1)}) fusion(s32[512]{0:T(512)S(1)} %iota_add_fusion.1), kind=kLoop, calls=%fused_computation.28 | loop fusion | flops 15728640 | bytes 5244928 | tf_op jit(solution)/shard_map/convert.6
  37.5 30.4 %collective-permute-done.1 = bf16[512,2,2560]{2,1,0:T(2,128)(2,1)} collective-permute-done((bf16[512,2,2560]{2,1,0:T(2,128)(2,1)}, bf16[512,2,2560]{2,1,0:T(2,128)(2,1)}, u32[]{:S(2)}, u32[]{:S(2)}) %collective-permute-start.1) | collective-permute-done | bytes 5242912 | tf_op jit(solution)/shard_map/ppermute | solution.py:22
  68.0 1.2 collective-permute-done
  69.2 0.0 copy-done.4
  69.2 64.1 %pad_maximum_fusion.1 = bf16[1536,2,2560]{2,1,0:T(2,128)(2,1)} fusion(bf16[512,2,2560]{2,1,0:T(2,128)(2,1)} %collective-permute-done.1, bf16[512,2,2560]{2,1,0:T(2,128)(2,1)S(1)} %copy-done.4, bf16[512,2,2560]{2,1,0:T(2,128)(2,1)} %collective-permute-done), kind=kLoop, calls=%fused_computation.14 | loop fusion | flops 15728640 | bytes 31457280 | tf_op jit(solution)/shard_map/concatenate | solution.py:23
  133.2 32.2 %reshape.90 = bf16[3072,2560]{1,0:T(8,128)(2,1)} reshape(bf16[1536,2,2560]{2,1,0:T(2,128)(2,1)} %pad_maximum_fusion.1) | data formatting | bytes 31457280 | tf_op jit(solution)/shard_map/reshape | solution.py:43
  165.4 20.0 %fusion.7 = f32[3072,1024]{1,0:T(8,128)S(1)} fusion(bf16[3072,2560]{1,0:T(8,128)(2,1)} %reshape.90, bf16[2560,512]{1,0:T(8,128)(2,1)} %get-tuple-element.16, bf16[2560,512]{1,0:T(8,128)(2,1)S(1)} %get-tuple-element.15), kind=kOutput, calls=%fused_computation.23 | convolution fusion | flops 16116613120 | bytes 33554432 | tf_op jit(solution)/shard_map/dot_general | solution.py:44
  185.5 0.9 fusion.30
  186.4 4.9 divide_convert_fusion.1
  191.2 5.7 %concatenate.29 = bf16[1536,2,512]{2,1,0:T(2,128)(2,1)} reshape(bf16[3072,512]{1,0:T(8,128)(2,1)} %get-tuple-element.10) | data formatting | bytes 6291456 | tf_op jit(solution)/shard_map/concatenate | solution.py:50
  197.0 2.8 pad_maximum_fusion.3
  199.8 3.2 concatenate.28
  203.0 0.0 copy-start
  203.0 4.3 slice.27
  207.3 0.0 copy-start.1
  207.3 5.2 slice_convert_fusion.1
  212.4 0.0 copy-done
  212.4 0.0 copy-done.1
  212.4 6.7 %pad_maximum_fusion.2 = bf16[1536,2,1024]{2,1,0:T(2,128)(2,1)} fusion(bf16[1536,2,512]{2,1,0:T(2,128)(2,1)S(1)} %copy-done, bf16[1536,2,512]{2,1,0:T(2,128)(2,1)S(1)} %copy-done.1), kind=kLoop, calls=%fused_computation.16 | loop fusion | flops 12582912 | bytes 12582912 | tf_op jit(solution)/shard_map/concatenate | solution.py:50
  219.1 63.7 %gather_fusion = bf16[4096,2,1024]{2,1,0:T(2,128)(2,1)} fusion(bf16[1536,2,1024]{2,1,0:T(2,128)(2,1)} %pad_maximum_fusion.2, s32[4096]{0:T(1024)S(1)} %broadcast_clamp_fusion), kind=kCustom, calls=%fused_computation | custom fusion | bytes 33570816 | tf_op jit(solution)/shard_map/jit(_take)/gather | solution.py:61
  282.9 0.0 copy-start.2
  282.9 0.0 copy-start.3
  282.9 20.2 %broadcast_select_fusion = bf16[512,8,2,1024]{3,2,1,0:T(2,128)(2,1)S(1)} fusion(bf16[512,8,2,1024]{3,2,1,0:T(2,128)(2,1)} %bitcast.17, pred[512,8]{1,0:T(8,128)(4,1)S(1)} %copy.7), kind=kLoop, calls=%fused_computation.2 | loop fusion | flops 8388608 | bytes 33558528 | tf_op jit(solution)/shard_map/jit(_take)/select_n | solution.py:61
  303.1 0.0 copy-done.2
  303.2 0.0 copy-done.3
  303.2 61.3 %fusion.1 = (bf16[512,8,512]{2,1,0:T(8,128)(2,1)}, bf16[512,8,512]{2,1,0:T(8,128)(2,1)}) fusion(f32[512,2,512]{2,1,0:T(2,128)S(1)} %copy-done.3, f32[512,2,512]{2,1,0:T(2,128)S(1)} %copy-done.2, bf16[512,8,2,1024]{3,2,1,0:T(2,128)(2,1)S(1)} %broadcast_select_fusion), kind=kLoop, calls=%fused_computation.8 | loop fusion | flops 37748736 | bytes 29360128 | tf_op jit(solution)/shard_map/reduce_sum | solution.py:69
  364.4 7.9 %pad_maximum_fusion = bf16[512,8,1024]{2,1,0:T(8,128)(2,1)} fusion(bf16[512,8,512]{2,1,0:T(8,128)(2,1)} %get-tuple-element.6, bf16[512,8,512]{2,1,0:T(8,128)(2,1)} %get-tuple-element.5), kind=kLoop, calls=%fused_computation.11 | loop fusion | flops 16777216 | bytes 16777216 | tf_op jit(solution)/shard_map/concatenate | solution.py:71
  372.3 8.0 %gather_fusion.1 = bf16[8,512,1024]{2,1,0:T(8,128)(2,1)} fusion(bf16[8,512,1024]{2,1,0:T(8,128)(2,1)} %bitcast.18, s32[1024]{0:T(1024)S(1)} %pad_clamp_fusion), kind=kCustom, calls=%fused_computation.1 | custom fusion | bytes 16777248 | tf_op jit(solution)/shard_map/jit(_take)/gather | solution.py:79
  380.3 7.6 %fusion.4 = bf16[4096,1024]{1,0:T(8,128)(2,1)} fusion(bf16[8,512,1024]{2,1,0:T(8,128)(2,1)} %gather_fusion.1, pred[4096]{0:T(1024)(128)(4,1)S(1)} %bitcast.20), kind=kLoop, calls=%fused_computation.13 | loop fusion | flops 4194304 | bytes 16781312 | tf_op jit(solution)/shard_map/convert_element_type | solution.py:85
  387.9 0.0 reduce-scatter.2.cloned.1.call-update
  387.9 3.3 fusion.25
  391.2 146.1 %reduce-scatter.2.cloned.1.call-done = bf16[512,1024]{1,0:T(8,128)(2,1)} async-done(((bf16[4096,1024]{1,0:T(8,128)(2,1)}), bf16[512,1024]{1,0:T(8,128)(2,1)}) %reduce-scatter.2.cloned.1.call-update) | async-done | bytes 1048592 | tf_op jit(solution)/shard_map/reduce_scatter | solution.py:84
  537.3 3.7 fusion.18
  (9 shorter events, 0.1 us)
Async XLA Ops:
  6.5 530.8 %reduce-scatter.2.cloned.1.call-start = ((), (), s32[]{:S(2)}) async-start(), calls=%async_computation.1 | async-start | bytes 9437184 | tf_op jit(solution)/shard_map/reduce_scatter | solution.py:84
  6.5 61.4 %collective-permute-start.1 = (bf16[512,2,2560]{2,1,0:T(2,128)(2,1)}, bf16[512,2,2560]{2,1,0:T(2,128)(2,1)}, u32[]{:S(2)}, u32[]{:S(2)}) collective-permute-start(bf16[512,2,2560]{2,1,0:T(2,128)(2,1)} %param.3), channel_id=1, source_target_pairs={{8,0},{16,8},{24,16},{9,1},{17,9},{25,17},{10,2},{18,10},{26,18},{... | collective-permute-start | bytes 15728648 | tf_op jit(solution)/shard_map/ppermute | solution.py:22
  9.1 60.0 %collective-permute-start = (bf16[512,2,2560]{2,1,0:T(2,128)(2,1)}, bf16[512,2,2560]{2,1,0:T(2,128)(2,1)}, u32[]{:S(2)}, u32[]{:S(2)}) collective-permute-start(bf16[512,2,2560]{2,1,0:T(2,128)(2,1)} %param.3), channel_id=1, source_target_pairs={{0,8},{8,16},{16,24},{1,9},{9,17},{17,25},{2,10},{10,18},{18,26},{... | collective-permute-start | bytes 15728648 | tf_op jit(solution)/shard_map/ppermute | solution.py:21
  13.4 55.8 %copy-start.4 = (bf16[512,2,2560]{2,1,0:T(2,128)(2,1)S(1)}, bf16[512,2,2560]{2,1,0:T(2,128)(2,1)}, u32[]{:S(2)}) copy-start(bf16[512,2,2560]{2,1,0:T(2,128)(2,1)} %param.3) | copy-start | bytes 15728644
  203.0 9.5 %copy-start = (bf16[1536,2,512]{2,1,0:T(2,128)(2,1)S(1)}, bf16[1536,2,512]{2,1,0:T(2,128)(2,1)}, u32[]{:S(2)}) copy-start(bf16[1536,2,512]{2,1,0:T(2,128)(2,1)} %concatenate.29) | copy-start | bytes 9437188
  207.3 5.2 copy-start.1
  282.9 20.3 %copy-start.2 = (f32[512,2,512]{2,1,0:T(2,128)S(1)}, f32[512,2,512]{2,1,0:T(2,128)}, u32[]{:S(2)}) copy-start(f32[512,2,512]{2,1,0:T(2,128)} %get-tuple-element.11) | copy-start | bytes 6291460
  282.9 20.3 %copy-start.3 = (f32[512,2,512]{2,1,0:T(2,128)S(1)}, f32[512,2,512]{2,1,0:T(2,128)}, u32[]{:S(2)}) copy-start(f32[512,2,512]{2,1,0:T(2,128)} %get-tuple-element.12) | copy-start | bytes 6291460
Sparse Core Ops, SparseCore 0:
  388.0 149.2 reduce-scatter.1
where the time goes:
time: 552 us; the launch traced here: 548 us
  other arithmetic  209 us (38%)
  waiting for transfers between devices  178 us (32%)
  local copies, waits for them, and re-layouts  118 us (21%)
  matrix products  23.7 us (4%)
  between operations  13.5 us (2%)
  starting transfers between devices  5.63 us (1%)
    reduce_scatter x1, waiting for transfers between devices, shards(): lax.psum_scatter(ordered.astype(jnp.bfloat16), 'tm', scatter_dimension=0,...  146 us
    concatenate x1, other arithmetic, extended(): array = jnp.concatenate([before, array, after], axis=dim)  64.1 us
    gather x1, local copies, waits for them, and re-layouts, shards(): jnp.take(whitened, local_rows, axis=0)  63.7 us
    reduce_sum x1, other arithmetic, shards(): cross_real = jnp.sum(own_real * far_real + own_imag * far_imag, axis=2)  61.3 us
    reshape x1, local copies, waits for them, and re-layouts, whiten(): flat = rows.reshape(-1, samples)  32.2 us
    ppermute x1, waiting for transfers between devices, extended(): after = lax.ppermute(first, axis, down)  30.4 us
    another operation x2, other arithmetic  27.9 us
    select_n x2, other arithmetic, shards(): jnp.take(whitened, local_rows, axis=0)  20.3 us
  transfers between devices with their start and end apart: 3, of which 3 were waited for; matrix products, arithmetic and copies ran while one was open for 5% of the time, Pallas kernels for 0%

commit v1 on v0

v1 whole, which is shorter than its diff:
```python
import functools
import math

import jax
import jax.numpy as jnp
import ml_dtypes
import numpy as np
from jax import lax
from jax.experimental import pallas as pl
from jax.experimental.pallas import tpu as pltpu
from jax.sharding import PartitionSpec as P

NFB = 512
F0 = 64
K = 8
LAG = 128
CHUNKS = 2
MESH = pl.DeviceIdType.MESH


def split(table):
    high = table.astype(ml_dtypes.bfloat16)
    low = (table - high.astype(np.float64)).astype(ml_dtypes.bfloat16)
    return high, low


def tables(samples):
    freqs = F0 + np.arange(NFB, dtype=np.int64)
    turn = 2.0 * math.pi / (2 * samples)
    angle = np.arange(samples, dtype=np.int64)[:, None] * freqs[None, :] % (2 * samples) * turn
    fourier = np.concatenate([np.cos(angle), -np.sin(angle)], axis=1).astype(ml_dtypes.bfloat16)
    shift = np.arange(LAG + 1, dtype=np.int64)[None, :]
    phi = freqs[:, None] * shift % (2 * samples) * turn
    cos_high, cos_low = split(np.cos(phi))
    sin_high, sin_low = split(np.sin(phi))
    cosine = np.concatenate([cos_high[:, :LAG], cos_low[:, :LAG]], axis=1)
    order = np.concatenate([[LAG], np.arange(1, LAG)])
    sine = np.concatenate([sin_high[:, order], sin_low[:, order]], axis=1)
    last = np.concatenate([np.tile(cos_high[:, LAG], (8, 1)), np.tile(cos_low[:, LAG], (8, 1))])
    return fourier, cosine, sine, last


def kernel(n_chan, n_tm, scale, rows_ref, owner_ref, x_hbm, f_hbm, cos_ref, sin_ref, last_ref, out_ref,
           x, table, spread, white, cr, ci, send, recv,
           load_sem, halo_send, halo_recv, lag_send, lag_recv):
    windows, block, samples = x.shape
    chan, me = lax.axis_index("chan"), lax.axis_index("tm")
    has_left, has_right = chan > 0, chan < n_chan - 1
    part = block // CHUNKS
    pairs = out_ref.shape[0]
    channels = pairs // K

    table_copy = pltpu.make_async_copy(f_hbm, table, load_sem.at[CHUNKS])
    loads = [
        pltpu.make_async_copy(
            x_hbm.at[:, pl.ds(c * part, part), :], x.at[:, pl.ds(c * part, part), :], load_sem.at[c]
        )
        for c in range(CHUNKS)
    ]
    loads[0].start()
    table_copy.start()
    for c in range(1, CHUNKS):
        loads[c].start()

    barrier = pltpu.get_barrier_semaphore()
    for s in range(1, n_tm):
        pl.semaphore_signal(barrier, inc=1, device_id=(chan, lax.rem(me + s, n_tm)), device_id_type=MESH)

    @pl.when(has_left)
    def _():
        pl.semaphore_signal(barrier, inc=1, device_id=(chan - 1, me), device_id_type=MESH)

    @pl.when(has_right)
    def _():
        pl.semaphore_signal(barrier, inc=1, device_id=(chan + 1, me), device_id_type=MESH)

    def halo(c, side):
        start = 2 * block if side == 0 else 0
        return pltpu.make_async_remote_copy(
            src_ref=white.at[pl.ds(block + c * part, part)],
            dst_ref=white.at[pl.ds(start + c * part, part)],
            send_sem=halo_send.at[side, c],
            recv_sem=halo_recv.at[side, c],
            device_id=(chan - 1 if side == 0 else chan + 1, me),
            device_id_type=MESH,
        )

    for c in range(CHUNKS):
        loads[c].wait()
        if c == 0:
            table_copy.wait()
        for w in range(windows):
            spectra = jnp.dot(x[w, c * part:(c + 1) * part, :], table[...], preferred_element_type=jnp.float32)
            real, imag = spectra[:, :NFB], spectra[:, NFB:]
            energy = real * real + imag * imag
            level = jnp.sum(energy, axis=1, keepdims=True) * (1.0 / NFB)
            factor = lax.rsqrt(energy + 0.1 * level + 1e-05)
            real, imag = real * factor, imag * factor
            for q in range(4):
                lanes = slice(q * 128, (q + 1) * 128)
                spread[pl.ds(w * 4 + q, part, stride=16), :] = real[:, lanes]
                spread[pl.ds(8 + w * 4 + q, part, stride=16), :] = imag[:, lanes]

        def pack(i, carry):
            tile = spread[pl.ds(pl.multiple_of(i * 256, 256), 256), :].reshape(16, 16, 128)
            white[pl.ds(block + c * part + i * 16, 16)] = tile.astype(jnp.bfloat16)
            return carry

        lax.fori_loop(0, part // 16, pack, 0)
        if c == 0:
            pl.semaphore_wait(barrier, n_tm - 1 + has_left.astype(jnp.int32) + has_right.astype(jnp.int32))

        @pl.when(has_left)
        def _():
            halo(c, 0).start()

        @pl.when(has_right)
        def _():
            halo(c, 1).start()

    @pl.when(has_left)
    def _():
        for c in range(CHUNKS):
            halo(c, 0).wait_send()
            halo(c, 1).wait_recv()

    @pl.when(has_right)
    def _():
        for c in range(CHUNKS):
            halo(c, 1).wait_send()
            halo(c, 0).wait_recv()

    def lag_copy(s):
        return pltpu.make_async_remote_copy(
            src_ref=send.at[s - 1],
            dst_ref=recv.at[s - 1],
            send_sem=lag_send.at[s - 1],
            recv_sem=lag_recv.at[s - 1],
            device_id=(chan, lax.rem(me + s, n_tm)),
            device_id_type=MESH,
        )

    def pair_block(s, carry):
        first = owner_ref[lax.rem(me + s, n_tm)] * channels

        def one_channel(i, inner):
            row = first + i
            own = white[block + row].astype(jnp.float32)
            own_real, own_imag = own[:8], own[8:]
            for k in range(K):
                far = white[rows_ref[row * K + k]].astype(jnp.float32)
                far_real, far_imag = far[:8], far[8:]
                at = pl.ds(pl.multiple_of(i * (8 * K) + 8 * k, 8), 8)
                cr[at, :] = own_real * far_real + own_imag * far_imag
                ci[at, :] = own_real * far_imag - own_imag * far_real
            return inner

        lax.fori_loop(0, channels, one_channel, 0, unroll=2)

        def gathered(ref):
            return jnp.concatenate(
                [
                    (ref[pl.ds(q, pairs, stride=8), :] + ref[pl.ds(q + 4, pairs, stride=8), :]).astype(jnp.bfloat16)
                    for q in range(4)
                ],
                axis=1,
            )

        real = gathered(cr)
        even = jnp.dot(real, cos_ref[...], preferred_element_type=jnp.float32)
        odd = jnp.dot(gathered(ci), sin_ref[...], preferred_element_type=jnp.float32)
        send[s - 1, :pairs, :LAG] = (even[:, :LAG] + even[:, LAG:]).astype(jnp.bfloat16)
        send[s - 1, :pairs, LAG:] = (odd[:, :LAG] + odd[:, LAG:]).astype(jnp.bfloat16)
        edge = lax.dot_general(
            last_ref[...], real, (((1,), (1,)), ((), ())), preferred_element_type=jnp.float32
        )
        edge = edge[:8] + edge[8:]
        pieces = [edge[:, q * 256:(q + 1) * 256] for q in range(pairs // 256)]
        send[s - 1, pairs:, :] = jnp.concatenate(pieces * (2 // len(pieces)), axis=0).astype(jnp.bfloat16)

        @pl.when(s < n_tm)
        def _():
            lag_copy(s).start()

        return carry

    lax.fori_loop(1, n_tm + 1, pair_block, 0)

    for s in range(1, n_tm):
        lag_copy(s).wait_recv()

    sub = lax.broadcasted_iota(jnp.int32, (128, 128), 0)
    lane = lax.broadcasted_iota(jnp.int32, (128, 128), 1)
    flip = jnp.where(sub + lane == LAG, 1.0, 0.0).astype(jnp.float32)

    def summed(rows):
        total = send[n_tm - 1, rows, :].astype(jnp.float32)
        for s in range(1, n_tm):
            total = total + recv[s - 1, rows, :].astype(jnp.float32)
        return total * scale

    edges = summed(slice(pairs, pairs + 16))
    for c in range(pairs // 128):
        total = summed(slice(c * 128, (c + 1) * 128))
        even, odd = total[:, :LAG], total[:, LAG:]
        at = c * 128 // 256 * 8
        edge = jnp.broadcast_to(edges[at:at + 1, c * 128 % 256:c * 128 % 256 + 128], (128, 128)).T
        odd_edge = odd[:, 0:1]
        odd = jnp.where(lane == 0, 0.0, odd)
        left = jnp.dot(
            even + odd, flip, precision=lax.Precision.HIGHEST, preferred_element_type=jnp.float32
        )
        rows = slice(c * 128, (c + 1) * 128)
        out_ref[rows, :LAG] = jnp.where(lane == 0, edge + odd_edge, left)
        out_ref[rows, LAG:2 * LAG] = even - odd
        out_ref[rows, 2 * LAG:] = edge[:, 0:1] - odd_edge

    for s in range(1, n_tm):
        lag_copy(s).wait_send()


def shards(n_chan, n_tm, constants, record, partners, block_owner):
    block, windows, samples = record.shape
    pairs = block * K // n_tm
    base = lax.axis_index("chan") * block - block
    rows = (partners - base).reshape(-1)
    count = jnp.arange(n_tm, dtype=jnp.int32)
    onehot = (block_owner[0][None, :] == count[:, None]).astype(jnp.int32)
    inverse = jnp.sum(onehot * count[None, :], axis=1)
    scale = 1.0 / math.sqrt(windows * n_tm * NFB)
    smem = pl.BlockSpec(memory_space=pltpu.SMEM)
    vmem = pl.BlockSpec(memory_space=pltpu.VMEM)
    anywhere = pl.BlockSpec(memory_space=pl.ANY)
    return pl.pallas_call(
        functools.partial(kernel, n_chan, n_tm, scale),
        out_shape=jax.ShapeDtypeStruct((pairs, 2 * LAG + 1), jnp.float32),
        in_specs=[smem, smem, anywhere, anywhere, vmem, vmem, vmem],
        out_specs=vmem,
        scratch_shapes=[
            pltpu.VMEM((windows, block, samples), jnp.bfloat16),
            pltpu.VMEM((samples, 2 * NFB), jnp.bfloat16),
            pltpu.VMEM((block // CHUNKS * 16, 128), jnp.float32),
            pltpu.VMEM((3 * block, 16, 128), jnp.bfloat16),
            pltpu.VMEM((pairs * 8, 128), jnp.float32),
            pltpu.VMEM((pairs * 8, 128), jnp.float32),
            pltpu.VMEM((n_tm, pairs + 16, 2 * LAG), jnp.bfloat16),
            pltpu.VMEM((n_tm - 1, pairs + 16, 2 * LAG), jnp.bfloat16),
            pltpu.SemaphoreType.DMA((CHUNKS + 1,)),
            pltpu.SemaphoreType.DMA((2, CHUNKS)),
            pltpu.SemaphoreType.DMA((2, CHUNKS)),
            pltpu.SemaphoreType.DMA((n_tm - 1,)),
            pltpu.SemaphoreType.DMA((n_tm - 1,)),
        ],
        compiler_params=pltpu.CompilerParams(
            collective_id=0, has_side_effects=True, vmem_limit_bytes=52 * 1024 * 1024
        ),
        cost_estimate=pl.CostEstimate(
            flops=2 * block * windows * samples * 2 * NFB, bytes_accessed=16 * 1024 * 1024, transcendentals=0
        ),
    )(rows, inverse, jnp.transpose(record, (1, 0, 2)), *(jnp.asarray(c) for c in constants))


def solution(mesh):
    placed = (P("chan", "tm", None), P("chan", None), P("chan", None))

    def run(record, partners, block_owner):
        body = functools.partial(shards, mesh.shape["chan"], mesh.shape["tm"], tables(record.shape[2]))
        return jax.shard_map(
            body, mesh=mesh, in_specs=placed, out_specs=P(("chan", "tm"), None), check_vma=False
        )(record, partners, block_owner)

    return run
```

time: 552 us -> 77.2 us (0.14)
  other arithmetic: 209 us -> 1.49 us
  waiting for transfers between devices: 178 us -> 0 us
  local copies, waits for them, and re-layouts: 118 us -> 6.97 us
  Pallas kernels: 0 us -> 68.5 us
  matrix products: 23.7 us -> 0 us
  between operations: 13.5 us -> 0.05 us
  starting transfers between devices: 5.63 us -> 0 us
    reduce_scatter x1 -> x0, waiting for transfers between devices: 146 us -> none  [shards(): lax.psum_scatter(ordered.astype(jnp.bfloat16), 'tm', scatter_dimension=0,...]
    concatenate x4 -> x0, other arithmetic: 81.4 us -> none  [the longest x1 64.1 us: extended(): array = jnp.concatenate([before, array, after], axis=dim)]
    gather x2 -> x0, local copies, waits for them, and re-layouts: 71.8 us -> none  [the longest x1 63.7 us: shards(): jnp.take(whitened, local_rows, axis=0)]
    pallas_call x0 -> x1, Pallas kernels: none -> 68.5 us  [shards(): pl.pallas_call(functools.partial(kernel, n_chan, n_tm, scale), out_shape=...]
    reduce_sum x3 -> x1, other arithmetic: 63.1 us -> 0.77 us  [shards(): inverse = jnp.sum(onehot * count[None, :], axis=1)]
    reshape x2 -> x1, local copies, waits for them, and re-layouts: 32.4 us -> 0.15 us  [shards(): rows = (partners - base).reshape(-1)]
    ppermute x2 -> x0, waiting for transfers between devices: 31.6 us -> none  [the longest x1 30.4 us: extended(): after = lax.ppermute(first, axis, down)]
    another operation x2 -> x0, other arithmetic: 27.9 us -> none
  transfers between devices with their start and end apart: 3 -> 0, of which waited for: 3 -> 0; matrix products, arithmetic and copies ran while one was open for 5% -> 0% of each run, Pallas kernels for 0% -> 0%
where the time goes in v1:
time: 77.2 us; the launch traced here: 77 us
  Pallas kernels  68.5 us (89%)
  local copies, waits for them, and re-layouts  6.97 us (9%)
  other arithmetic  1.49 us (2%)
    pallas_call x1, Pallas kernels, shards(): pl.pallas_call(functools.partial(kernel, n_chan, n_tm, scale), out_shape=...  68.5 us
    unnamed x7, local copies, waits for them, and re-layouts  5.66 us

profile of v1, /device:TPU:11, one launch (start us, length us, event | category | flops | bytes accessed | tf_op | source)
XLA Modules:
  0.0 77.0 jit_solution(16054346023048666405)
XLA Ops:
  0.0 0.8 select_reduce_fusion.owner_ref
  0.8 0.7 broadcast_subtract_fusion
  1.5 0.1 copy.13
  1.6 0.2 reshape.3.rows_ref
  1.8 0.0 copy-start
  1.8 0.0 copy-start.1
  1.8 0.0 copy-start.2
  1.8 5.6 %copy.17 = bf16[512,2,2560]{2,0,1:T(8,128)(2,1)} copy(bf16[512,2,2560]{2,1,0:T(2,128)(2,1)} %param.7) | data formatting | bytes 10485760 | tf_op args[0]
  7.5 0.0 copy-done
  7.5 0.0 copy-done.1
  7.5 0.0 copy-done.2
  7.5 68.5 %shard_map.73 = f32[512,257]{1,0:T(8,128)S(1)} custom-call(s32[4096]{0:T(1024)S(1)} %reshape.3.rows_ref, s32[8]{0:T(128)S(1)} %select_reduce_fusion.owner_ref, bf16[2,512,2560]{2,1,0:T(8,128)(2,1)} %bitcast.4, bf16[2560,1024]{1,0:T(8,128)(2,1)} %constant.20.clone.f_hbm, bf16[512,256]{1,0:T(8,128)(2,1)S(1)} %copy-done.1, bf16[512,256]{1,0:T(8,128)(2,1)S(1)} %copy-done, ...), custom_call_target="tpu_custom_call" | custom-call | flops 5368709120 | bytes 16777216 | tf_op jit(solution)/shard_map/pallas_call | solution.py:234
  75.9 1.0 %copy.15 = f32[512,257]{0,1:T(8,128)} copy(f32[512,257]{1,0:T(8,128)S(1)} %shard_map.73) | data formatting | bytes 1052672 | tf_op jit(solution)/shard_map/pallas_call | solution.py:234
Async XLA Ops:
  1.8 5.7 %copy-start = (bf16[512,256]{1,0:T(8,128)(2,1)S(1)}, bf16[512,256]{1,0:T(8,128)(2,1)}, u32[]{:S(2)}) copy-start(bf16[512,256]{1,0:T(8,128)(2,1)} %constant.22.clone.sin_ref) | copy-start | bytes 786436
  1.8 5.7 %copy-start.1 = (bf16[512,256]{1,0:T(8,128)(2,1)S(1)}, bf16[512,256]{1,0:T(8,128)(2,1)}, u32[]{:S(2)}) copy-start(bf16[512,256]{1,0:T(8,128)(2,1)} %constant.21.clone.cos_ref) | copy-start | bytes 786436
  1.8 5.7 %copy-start.2 = (bf16[16,512]{1,0:T(8,128)(2,1)S(1)}, bf16[16,512]{1,0:T(8,128)(2,1)}, u32[]{:S(2)}) copy-start(bf16[16,512]{1,0:T(8,128)(2,1)} %constant.23.clone.last_ref) | copy-start | bytes 49156

commit v2 on v1

--- a/solution.py
+++ b/solution.py
@@ -140,27 +140,40 @@
             device_id_type=MESH,
         )
 
+    base = chan * block - block
+    upper = lax.broadcasted_iota(jnp.int32, (8, 128), 0) < 4
+
+    def both_windows(first, second):
+        return jnp.where(upper, first, second) + pltpu.roll(jnp.where(upper, second, first), 4, 0)
+
     def pair_block(s, carry):
-        first = owner_ref[lax.rem(me + s, n_tm)] * channels
+        target = lax.rem(me + s, n_tm)
+        first = jnp.int32(0)
+        for j in range(n_tm):
+            first = jnp.where(owner_ref[0, j] == target, j * channels, first)
 
         def one_channel(i, inner):
             row = first + i
             own = white[block + row].astype(jnp.float32)
             own_real, own_imag = own[:8], own[8:]
-            for k in range(K):
-                far = white[rows_ref[row * K + k]].astype(jnp.float32)
-                far_real, far_imag = far[:8], far[8:]
-                at = pl.ds(pl.multiple_of(i * (8 * K) + 8 * k, 8), 8)
-                cr[at, :] = own_real * far_real + own_imag * far_imag
-                ci[at, :] = own_real * far_imag - own_imag * far_real
+            for k in range(0, K, 2):
+                real, imag = [], []
+                for far_slot in (k, k + 1):
+                    far = white[jnp.maximum(rows_ref[far_slot, row] - base, 0)].astype(jnp.float32)
+                    far_real, far_imag = far[:8], far[8:]
+                    real.append(own_real * far_real + own_imag * far_imag)
+                    imag.append(own_real * far_imag - own_imag * far_real)
+                at = pl.ds(pl.multiple_of(i * (4 * K) + 4 * k, 8), 8)
+                cr[at, :] = both_windows(*real)
+                ci[at, :] = both_windows(*imag)
             return inner
 
-        lax.fori_loop(0, channels, one_channel, 0, unroll=2)
+        lax.fori_loop(0, channels, one_channel, 0, unroll=4)
 
         def gathered(ref):
             return jnp.concatenate(
                 [
-                    (ref[pl.ds(q, pairs, stride=8), :] + ref[pl.ds(q + 4, pairs, stride=8), :]).astype(jnp.bfloat16)
+                    ref[pl.ds(q, pairs, stride=4), :].astype(jnp.bfloat16)
                     for q in range(4)
                 ],
                 axis=1,
@@ -222,11 +235,6 @@
 def shards(n_chan, n_tm, constants, record, partners, block_owner):
     block, windows, samples = record.shape
     pairs = block * K // n_tm
-    base = lax.axis_index("chan") * block - block
-    rows = (partners - base).reshape(-1)
-    count = jnp.arange(n_tm, dtype=jnp.int32)
-    onehot = (block_owner[0][None, :] == count[:, None]).astype(jnp.int32)
-    inverse = jnp.sum(onehot * count[None, :], axis=1)
     scale = 1.0 / math.sqrt(windows * n_tm * NFB)
     smem = pl.BlockSpec(memory_space=pltpu.SMEM)
     vmem = pl.BlockSpec(memory_space=pltpu.VMEM)
@@ -241,8 +249,8 @@
             pltpu.VMEM((samples, 2 * NFB), jnp.bfloat16),
             pltpu.VMEM((block // CHUNKS * 16, 128), jnp.float32),
             pltpu.VMEM((3 * block, 16, 128), jnp.bfloat16),
-            pltpu.VMEM((pairs * 8, 128), jnp.float32),
-            pltpu.VMEM((pairs * 8, 128), jnp.float32),
+            pltpu.VMEM((pairs * 4, 128), jnp.float32),
+            pltpu.VMEM((pairs * 4, 128), jnp.float32),
             pltpu.VMEM((n_tm, pairs + 16, 2 * LAG), jnp.bfloat16),
             pltpu.VMEM((n_tm - 1, pairs + 16, 2 * LAG), jnp.bfloat16),
             pltpu.SemaphoreType.DMA((CHUNKS + 1,)),
@@ -257,7 +265,7 @@
         cost_estimate=pl.CostEstimate(
             flops=2 * block * windows * samples * 2 * NFB, bytes_accessed=16 * 1024 * 1024, transcendentals=0
         ),
-    )(rows, inverse, jnp.transpose(record, (1, 0, 2)), *(jnp.asarray(c) for c in constants))
+    )(jnp.transpose(partners), block_owner, jnp.transpose(record, (1, 0, 2)), *(jnp.asarray(c) for c in constants))
 
 
 def solution(mesh):

time: 77.2 us -> 75.7 us (0.981)
  other arithmetic: 1.49 us -> 0 us
    unnamed x7 -> x11, local copies, waits for them, and re-layouts: 5.66 us -> 5.66 us
where the time goes in v2:
time: 75.7 us; the launch traced here: 75.6 us
  Pallas kernels  68.8 us (91%)
  local copies, waits for them, and re-layouts  6.7 us (9%)
    pallas_call x1, Pallas kernels, shards(): pl.pallas_call(functools.partial(kernel, n_chan, n_tm, scale), out_shape=...  68.8 us
    unnamed x11, local copies, waits for them, and re-layouts  5.66 us

profile of v2, /device:TPU:11, one launch (start us, length us, event | category | flops | bytes accessed | tf_op | source)
XLA Modules:
  0.0 75.6 jit_solution(4196415117096568561)
XLA Ops:
  0.0 0.0 copy-start
  0.0 0.0 copy-start.1
  0.0 0.0 copy-start.2
  0.0 0.0 copy-start.3
  0.0 0.0 copy-start.4
  0.0 5.6 %copy.11 = bf16[512,2,2560]{2,0,1:T(8,128)(2,1)} copy(bf16[512,2,2560]{2,1,0:T(2,128)(2,1)} %param.7) | data formatting | bytes 10485760 | tf_op args[0]
  5.7 0.0 copy-done
  5.7 0.0 copy-done.1
  5.7 0.0 copy-done.2
  5.7 0.0 copy-done.3
  5.7 0.0 copy-done.4
  5.7 68.8 %shard_map.73 = f32[512,257]{1,0:T(8,128)S(1)} custom-call(s32[8,512]{1,0:T(8,128)S(1)} %bitcast.4, s32[1,8]{1,0:T(1,128)S(1)} %copy-done.1, bf16[2,512,2560]{2,1,0:T(8,128)(2,1)} %bitcast.5, bf16[2560,1024]{1,0:T(8,128)(2,1)} %constant.8.clone.f_hbm, bf16[512,256]{1,0:T(8,128)(2,1)S(1)} %copy-done.3, bf16[512,256]{1,0:T(8,128)(2,1)S(1)} %copy-done.2, ...), custom_call_target="tpu_custom_call" | custom-call | flops 5368709120 | bytes 16777216 | tf_op jit(solution)/shard_map/pallas_call | solution.py:242
  74.5 1.0 %copy.9 = f32[512,257]{0,1:T(8,128)} copy(f32[512,257]{1,0:T(8,128)S(1)} %shard_map.73) | data formatting | bytes 1052672 | tf_op jit(solution)/shard_map/pallas_call | solution.py:242
Async XLA Ops:
  0.0 5.7 %copy-start = (s32[512,8]{0,1:T(8,128)S(1)}, s32[512,8]{0,1:T(8,128)}, u32[]{:S(2)}) copy-start(s32[512,8]{0,1:T(8,128)} %param.8) | copy-start | bytes 49156
  0.0 5.7 %copy-start.1 = (s32[1,8]{1,0:T(1,128)S(1)}, s32[1,8]{1,0:T(1,128)}, u32[]{:S(2)}) copy-start(s32[1,8]{1,0:T(1,128)} %owner_ref.1) | copy-start | bytes 100
  0.0 5.7 %copy-start.2 = (bf16[512,256]{1,0:T(8,128)(2,1)S(1)}, bf16[512,256]{1,0:T(8,128)(2,1)}, u32[]{:S(2)}) copy-start(bf16[512,256]{1,0:T(8,128)(2,1)} %constant.10.clone.sin_ref) | copy-start | bytes 786436
  0.0 5.7 %copy-start.3 = (bf16[512,256]{1,0:T(8,128)(2,1)S(1)}, bf16[512,256]{1,0:T(8,128)(2,1)}, u32[]{:S(2)}) copy-start(bf16[512,256]{1,0:T(8,128)(2,1)} %constant.9.clone.cos_ref) | copy-start | bytes 786436
  0.0 5.7 %copy-start.4 = (bf16[16,512]{1,0:T(8,128)(2,1)S(1)}, bf16[16,512]{1,0:T(8,128)(2,1)}, u32[]{:S(2)}) copy-start(bf16[16,512]{1,0:T(8,128)(2,1)} %constant.11.clone.last_ref) | copy-start | bytes 49156

commit v3 on v2

--- a/solution.py
+++ b/solution.py
@@ -41,10 +41,13 @@
 
 
 def kernel(n_chan, n_tm, scale, rows_ref, owner_ref, x_hbm, f_hbm, cos_ref, sin_ref, last_ref, out_ref,
-           x, table, spread, white, cr, ci, send, recv,
-           load_sem, halo_send, halo_recv, lag_send, lag_recv):
+           x, table, spread, white, cr, ci, mine, fold_out, fold_in, send, recv,
+           load_sem, halo_send, halo_recv, fold_send, fold_recv, lag_send, lag_recv):
     windows, block, samples = x.shape
     chan, me = lax.axis_index("chan"), lax.axis_index("tm")
+    half = n_tm // 2
+    side = lax.rem(me, 2)
+    mate = me + 1 - 2 * side
     has_left, has_right = chan > 0, chan < n_chan - 1
     part = block // CHUNKS
     pairs = out_ref.shape[0]
@@ -63,8 +66,9 @@
         loads[c].start()
 
     barrier = pltpu.get_barrier_semaphore()
-    for s in range(1, n_tm):
-        pl.semaphore_signal(barrier, inc=1, device_id=(chan, lax.rem(me + s, n_tm)), device_id_type=MESH)
+    pl.semaphore_signal(barrier, inc=1, device_id=(chan, mate), device_id_type=MESH)
+    for s in range(1, half):
+        pl.semaphore_signal(barrier, inc=1, device_id=(chan, lax.rem(me + 2 * s, n_tm)), device_id_type=MESH)
 
     @pl.when(has_left)
     def _():
@@ -74,14 +78,14 @@
     def _():
         pl.semaphore_signal(barrier, inc=1, device_id=(chan + 1, me), device_id_type=MESH)
 
-    def halo(c, side):
-        start = 2 * block if side == 0 else 0
+    def halo(c, way):
+        start = 2 * block if way == 0 else 0
         return pltpu.make_async_remote_copy(
             src_ref=white.at[pl.ds(block + c * part, part)],
             dst_ref=white.at[pl.ds(start + c * part, part)],
-            send_sem=halo_send.at[side, c],
-            recv_sem=halo_recv.at[side, c],
-            device_id=(chan - 1 if side == 0 else chan + 1, me),
+            send_sem=halo_send.at[way, c],
+            recv_sem=halo_recv.at[way, c],
+            device_id=(chan - 1 if way == 0 else chan + 1, me),
             device_id_type=MESH,
         )
 
@@ -108,7 +112,7 @@
 
         lax.fori_loop(0, part // 16, pack, 0)
         if c == 0:
-            pl.semaphore_wait(barrier, n_tm - 1 + has_left.astype(jnp.int32) + has_right.astype(jnp.int32))
+            pl.semaphore_wait(barrier, half + has_left.astype(jnp.int32) + has_right.astype(jnp.int32))
 
         @pl.when(has_left)
         def _():
@@ -129,6 +133,16 @@
         for c in range(CHUNKS):
             halo(c, 1).wait_send()
             halo(c, 0).wait_recv()
+
+    def fold_copy(s):
+        return pltpu.make_async_remote_copy(
+            src_ref=fold_out.at[s - 1],
+            dst_ref=fold_in.at[s - 1],
+            send_sem=fold_send.at[s - 1],
+            recv_sem=fold_recv.at[s - 1],
+            device_id=(chan, mate),
+            device_id_type=MESH,
+        )
 
     def lag_copy(s):
         return pltpu.make_async_remote_copy(
@@ -136,7 +150,7 @@
             dst_ref=recv.at[s - 1],
             send_sem=lag_send.at[s - 1],
             recv_sem=lag_recv.at[s - 1],
-            device_id=(chan, lax.rem(me + s, n_tm)),
+            device_id=(chan, lax.rem(me + 2 * s, n_tm)),
             device_id_type=MESH,
         )
 
@@ -146,8 +160,7 @@
     def both_windows(first, second):
         return jnp.where(upper, first, second) + pltpu.roll(jnp.where(upper, second, first), 4, 0)
 
-    def pair_block(s, carry):
-        target = lax.rem(me + s, n_tm)
+    def pair_block(target, out):
         first = jnp.int32(0)
         for j in range(n_tm):
             first = jnp.where(owner_ref[0, j] == target, j * channels, first)
@@ -182,24 +195,32 @@
         real = gathered(cr)
         even = jnp.dot(real, cos_ref[...], preferred_element_type=jnp.float32)
         odd = jnp.dot(gathered(ci), sin_ref[...], preferred_element_type=jnp.float32)
-        send[s - 1, :pairs, :LAG] = (even[:, :LAG] + even[:, LAG:]).astype(jnp.bfloat16)
-        send[s - 1, :pairs, LAG:] = (odd[:, :LAG] + odd[:, LAG:]).astype(jnp.bfloat16)
+        out[:pairs, :LAG] = (even[:, :LAG] + even[:, LAG:]).astype(out.dtype)
+        out[:pairs, LAG:] = (odd[:, :LAG] + odd[:, LAG:]).astype(out.dtype)
         edge = lax.dot_general(
             last_ref[...], real, (((1,), (1,)), ((), ())), preferred_element_type=jnp.float32
         )
         edge = edge[:8] + edge[8:]
         pieces = [edge[:, q * 256:(q + 1) * 256] for q in range(pairs // 256)]
-        send[s - 1, pairs:, :] = jnp.concatenate(pieces * (2 // len(pieces)), axis=0).astype(jnp.bfloat16)
-
-        @pl.when(s < n_tm)
+        out[pairs:, :] = jnp.concatenate(pieces * (2 // len(pieces)), axis=0).astype(out.dtype)
+
+    def step(s, carry):
+        target = lax.rem(me + 2 * s, n_tm)
+        pair_block(target + 1 - 2 * side, fold_out.at[s - 1])
+        fold_copy(s).start()
+
+        @pl.when(s > 1)
         def _():
-            lag_copy(s).start()
-
+            fold_copy(s - 1).wait_recv()
+            send[s - 2] = (mine[...] + fold_in[s - 2].astype(jnp.float32)).astype(jnp.bfloat16)
+            lag_copy(s - 1).start()
+
+        pair_block(target, mine)
         return carry
 
-    lax.fori_loop(1, n_tm + 1, pair_block, 0)
-
-    for s in range(1, n_tm):
+    lax.fori_loop(1, half + 1, step, 0)
+    fold_copy(half).wait_recv()
+    for s in range(1, half):
         lag_copy(s).wait_recv()
 
     sub = lax.broadcasted_iota(jnp.int32, (128, 128), 0)
@@ -207,8 +228,8 @@
     flip = jnp.where(sub + lane == LAG, 1.0, 0.0).astype(jnp.float32)
 
     def summed(rows):
-        total = send[n_tm - 1, rows, :].astype(jnp.float32)
-        for s in range(1, n_tm):
+        total = mine[rows, :] + fold_in[half - 1, rows, :].astype(jnp.float32)
+        for s in range(1, half):
             total = total + recv[s - 1, rows, :].astype(jnp.float32)
         return total * scale
 
@@ -228,8 +249,10 @@
         out_ref[rows, LAG:2 * LAG] = even - odd
         out_ref[rows, 2 * LAG:] = edge[:, 0:1] - odd_edge
 
-    for s in range(1, n_tm):
+    for s in range(1, half):
         lag_copy(s).wait_send()
+    for s in range(1, half + 1):
+        fold_copy(s).wait_send()
 
 
 def shards(n_chan, n_tm, constants, record, partners, block_owner):
@@ -251,13 +274,18 @@
             pltpu.VMEM((3 * block, 16, 128), jnp.bfloat16),
             pltpu.VMEM((pairs * 4, 128), jnp.float32),
             pltpu.VMEM((pairs * 4, 128), jnp.float32),
-            pltpu.VMEM((n_tm, pairs + 16, 2 * LAG), jnp.bfloat16),
-            pltpu.VMEM((n_tm - 1, pairs + 16, 2 * LAG), jnp.bfloat16),
+            pltpu.VMEM((pairs + 16, 2 * LAG), jnp.float32),
+            pltpu.VMEM((n_tm // 2, pairs + 16, 2 * LAG), jnp.bfloat16),
+            pltpu.VMEM((n_tm // 2, pairs + 16, 2 * LAG), jnp.bfloat16),
+            pltpu.VMEM((n_tm // 2 - 1, pairs + 16, 2 * LAG), jnp.bfloat16),
+            pltpu.VMEM((n_tm // 2 - 1, pairs + 16, 2 * LAG), jnp.bfloat16),
             pltpu.SemaphoreType.DMA((CHUNKS + 1,)),
             pltpu.SemaphoreType.DMA((2, CHUNKS)),
             pltpu.SemaphoreType.DMA((2, CHUNKS)),
-            pltpu.SemaphoreType.DMA((n_tm - 1,)),
-            pltpu.SemaphoreType.DMA((n_tm - 1,)),
+            pltpu.SemaphoreType.DMA((n_tm // 2,)),
+            pltpu.SemaphoreType.DMA((n_tm // 2,)),
+            pltpu.SemaphoreType.DMA((n_tm // 2 - 1,)),
+            pltpu.SemaphoreType.DMA((n_tm // 2 - 1,)),
         ],
         compiler_params=pltpu.CompilerParams(
             collective_id=0, has_side_effects=True, vmem_limit_bytes=52 * 1024 * 1024

time: 75.7 us -> 63.9 us (0.84)
  the two profiles are of different devices: /device:TPU:11 before, /device:TPU:1 now
where the time goes in v3:
time: 63.9 us; the launch traced here: 63.8 us
  Pallas kernels  57 us (89%)
  local copies, waits for them, and re-layouts  6.7 us (10%)
    pallas_call x1, Pallas kernels, shards(): pl.pallas_call(functools.partial(kernel, n_chan, n_tm, scale), out_shape=...  57 us
    unnamed x11, local copies, waits for them, and re-layouts  5.66 us

profile of v3, /device:TPU:1, one launch (start us, length us, event | category | flops | bytes accessed | tf_op | source)
XLA Modules:
  0.0 63.8 jit_solution(4067605081596302677)
XLA Ops:
  0.0 0.0 copy-start
  0.0 0.0 copy-start.1
  0.0 0.0 copy-start.2
  0.0 0.0 copy-start.3
  0.0 0.0 copy-start.4
  0.0 5.6 %copy.11 = bf16[512,2,2560]{2,0,1:T(8,128)(2,1)} copy(bf16[512,2,2560]{2,1,0:T(2,128)(2,1)} %param.7) | data formatting | bytes 10485760 | tf_op args[0]
  5.7 0.0 copy-done
  5.7 0.0 copy-done.1
  5.7 0.0 copy-done.2
  5.7 0.0 copy-done.3
  5.7 0.0 copy-done.4
  5.7 57.0 %shard_map.73 = f32[512,257]{1,0:T(8,128)S(1)} custom-call(s32[8,512]{1,0:T(8,128)S(1)} %bitcast.4, s32[1,8]{1,0:T(1,128)S(1)} %copy-done.1, bf16[2,512,2560]{2,1,0:T(8,128)(2,1)} %bitcast.5, bf16[2560,1024]{1,0:T(8,128)(2,1)} %constant.8.clone.f_hbm, bf16[512,256]{1,0:T(8,128)(2,1)S(1)} %copy-done.3, bf16[512,256]{1,0:T(8,128)(2,1)S(1)} %copy-done.2, ...), custom_call_target="tpu_custom_call" | custom-call | flops 5368709120 | bytes 16777216 | tf_op jit(solution)/shard_map/pallas_call | solution.py:265
  62.7 1.0 %copy.9 = f32[512,257]{0,1:T(8,128)} copy(f32[512,257]{1,0:T(8,128)S(1)} %shard_map.73) | data formatting | bytes 1052672 | tf_op jit(solution)/shard_map/pallas_call | solution.py:265
Async XLA Ops:
  0.0 5.7 %copy-start = (s32[512,8]{0,1:T(8,128)S(1)}, s32[512,8]{0,1:T(8,128)}, u32[]{:S(2)}) copy-start(s32[512,8]{0,1:T(8,128)} %param.8) | copy-start | bytes 49156
  0.0 5.7 %copy-start.1 = (s32[1,8]{1,0:T(1,128)S(1)}, s32[1,8]{1,0:T(1,128)}, u32[]{:S(2)}) copy-start(s32[1,8]{1,0:T(1,128)} %owner_ref.1) | copy-start | bytes 100
  0.0 5.7 %copy-start.2 = (bf16[512,256]{1,0:T(8,128)(2,1)S(1)}, bf16[512,256]{1,0:T(8,128)(2,1)}, u32[]{:S(2)}) copy-start(bf16[512,256]{1,0:T(8,128)(2,1)} %constant.10.clone.sin_ref) | copy-start | bytes 786436
  0.0 5.7 %copy-start.3 = (bf16[512,256]{1,0:T(8,128)(2,1)S(1)}, bf16[512,256]{1,0:T(8,128)(2,1)}, u32[]{:S(2)}) copy-start(bf16[512,256]{1,0:T(8,128)(2,1)} %constant.9.clone.cos_ref) | copy-start | bytes 786436
  0.0 5.7 %copy-start.4 = (bf16[16,512]{1,0:T(8,128)(2,1)S(1)}, bf16[16,512]{1,0:T(8,128)(2,1)}, u32[]{:S(2)}) copy-start(bf16[16,512]{1,0:T(8,128)(2,1)} %constant.11.clone.last_ref) | copy-start | bytes 49156

commit v4 on v3

--- a/solution.py
+++ b/solution.py
@@ -14,7 +14,8 @@
 F0 = 64
 K = 8
 LAG = 128
-CHUNKS = 2
+CHUNKS = 4
+GAIN = 1.45
 MESH = pl.DeviceIdType.MESH
 
 
@@ -31,8 +32,8 @@
     fourier = np.concatenate([np.cos(angle), -np.sin(angle)], axis=1).astype(ml_dtypes.bfloat16)
     shift = np.arange(LAG + 1, dtype=np.int64)[None, :]
     phi = freqs[:, None] * shift % (2 * samples) * turn
-    cos_high, cos_low = split(np.cos(phi))
-    sin_high, sin_low = split(np.sin(phi))
+    cos_high, cos_low = split(GAIN * np.cos(phi))
+    sin_high, sin_low = split(GAIN * np.sin(phi))
     cosine = np.concatenate([cos_high[:, :LAG], cos_low[:, :LAG]], axis=1)
     order = np.concatenate([[LAG], np.arange(1, LAG)])
     sine = np.concatenate([sin_high[:, order], sin_low[:, order]], axis=1)
@@ -258,7 +259,7 @@
 def shards(n_chan, n_tm, constants, record, partners, block_owner):
     block, windows, samples = record.shape
     pairs = block * K // n_tm
-    scale = 1.0 / math.sqrt(windows * n_tm * NFB)
+    scale = 1.0 / (GAIN * math.sqrt(windows * n_tm * NFB))
     smem = pl.BlockSpec(memory_space=pltpu.SMEM)
     vmem = pl.BlockSpec(memory_space=pltpu.VMEM)
     anywhere = pl.BlockSpec(memory_space=pl.ANY)

time: 63.9 us -> 61.9 us (0.969)
  Pallas kernels: 57 us -> 55 us
    pallas_call x1, Pallas kernels: 57 us -> 55 us  [shards(): pl.pallas_call(functools.partial(kernel, n_chan, n_tm, scale), out_shape=...]
where the time goes in v4:
time: 61.9 us; the launch traced here: 61.8 us
  Pallas kernels  55 us (89%)
  local copies, waits for them, and re-layouts  6.7 us (11%)
    pallas_call x1, Pallas kernels, shards(): pl.pallas_call(functools.partial(kernel, n_chan, n_tm, scale), out_shape=...  55 us
    unnamed x11, local copies, waits for them, and re-layouts  5.66 us

profile of v4, /device:TPU:1, one launch (start us, length us, event | category | flops | bytes accessed | tf_op | source)
XLA Modules:
  0.0 61.8 jit_solution(1631959174283109887)
XLA Ops:
  0.0 0.0 copy-start
  0.0 0.0 copy-start.1
  0.0 0.0 copy-start.2
  0.0 0.0 copy-start.3
  0.0 0.0 copy-start.4
  0.0 5.6 %copy.11 = bf16[512,2,2560]{2,0,1:T(8,128)(2,1)} copy(bf16[512,2,2560]{2,1,0:T(2,128)(2,1)} %param.7) | data formatting | bytes 10485760 | tf_op args[0]
  5.7 0.0 copy-done
  5.7 0.0 copy-done.1
  5.7 0.0 copy-done.2
  5.7 0.0 copy-done.3
  5.7 0.0 copy-done.4
  5.7 55.0 %shard_map.73 = f32[512,257]{1,0:T(8,128)S(1)} custom-call(s32[8,512]{1,0:T(8,128)S(1)} %bitcast.4, s32[1,8]{1,0:T(1,128)S(1)} %copy-done.1, bf16[2,512,2560]{2,1,0:T(8,128)(2,1)} %bitcast.5, bf16[2560,1024]{1,0:T(8,128)(2,1)} %constant.8.clone.f_hbm, bf16[512,256]{1,0:T(8,128)(2,1)S(1)} %copy-done.3, bf16[512,256]{1,0:T(8,128)(2,1)S(1)} %copy-done.2, ...), custom_call_target="tpu_custom_call" | custom-call | flops 5368709120 | bytes 16777216 | tf_op jit(solution)/shard_map/pallas_call | solution.py:266
  60.8 1.0 %copy.9 = f32[512,257]{0,1:T(8,128)} copy(f32[512,257]{1,0:T(8,128)S(1)} %shard_map.73) | data formatting | bytes 1052672 | tf_op jit(solution)/shard_map/pallas_call | solution.py:266
Async XLA Ops:
  0.0 5.7 %copy-start = (s32[512,8]{0,1:T(8,128)S(1)}, s32[512,8]{0,1:T(8,128)}, u32[]{:S(2)}) copy-start(s32[512,8]{0,1:T(8,128)} %param.8) | copy-start | bytes 49156
  0.0 5.7 %copy-start.1 = (s32[1,8]{1,0:T(1,128)S(1)}, s32[1,8]{1,0:T(1,128)}, u32[]{:S(2)}) copy-start(s32[1,8]{1,0:T(1,128)} %owner_ref.1) | copy-start | bytes 100
  0.0 5.7 %copy-start.2 = (bf16[512,256]{1,0:T(8,128)(2,1)S(1)}, bf16[512,256]{1,0:T(8,128)(2,1)}, u32[]{:S(2)}) copy-start(bf16[512,256]{1,0:T(8,128)(2,1)} %constant.10.clone.sin_ref) | copy-start | bytes 786436
  0.0 5.7 %copy-start.3 = (bf16[512,256]{1,0:T(8,128)(2,1)S(1)}, bf16[512,256]{1,0:T(8,128)(2,1)}, u32[]{:S(2)}) copy-start(bf16[512,256]{1,0:T(8,128)(2,1)} %constant.9.clone.cos_ref) | copy-start | bytes 786436
  0.0 5.7 %copy-start.4 = (bf16[16,512]{1,0:T(8,128)(2,1)S(1)}, bf16[16,512]{1,0:T(8,128)(2,1)}, u32[]{:S(2)}) copy-start(bf16[16,512]{1,0:T(8,128)(2,1)} %constant.11.clone.last_ref) | copy-start | bytes 49156
